TPU v7x, 256 devices: a whole 4x4x8 slice. The times are simulated.
256 devices in a mesh: ctx: 64 (over y, x_lo, z), dp: 4 (over x_hi, core).
Axes of the slice: x: 4 (x_hi: 2, x_lo: 2; x = x_hi * 2 + x_lo), y: 4, z: 8, core: 2. Of those that a mesh axis runs over, the one named last changes fastest.
Arguments:
- all_query_heads: bfloat16 [4, 8192, 4096], P('dp', 'ctx'), may hold values from -32 to 32
- grouped_key_heads: bfloat16 [4, 8192, 512], P('dp', 'ctx'), may hold values from -32 to 32
- grouped_value_heads: bfloat16 [4, 8192, 512], P('dp', 'ctx'), may hold values from -5 to 5
- output_gradient: bfloat16 [4, 8192, 4096], P('dp', 'ctx'), may hold values from -72 to 72
- head_ordering: int32 [4, 4], P('dp'), may hold values from 0 to 3, each once within a row
- adapter_activations: bfloat16 [4, 8192, 48], P('dp', 'ctx'), may hold values from -0.03125 to 0.03125
Outputs:
- query_gradient: bfloat16 [4, 8192, 4096], P('dp', 'ctx')
- key_gradient: bfloat16 [4, 8192, 512], P('dp', 'ctx')
- value_gradient: bfloat16 [4, 8192, 512], P('dp', 'ctx')
- adapter_query_gradient: float32 [16, 4096], P(None, ('ctx', 'dp'))
- adapter_key_value_gradient: float32 [16, 1024], P(None, ('ctx', 'dp'))
Inputs may be any that keep to these rules, and one draw needn't show every extreme that they name: `head_ordering`: each row names each key-value head once.
All inputs are finite; a program needn't handle non-finite values.
Results may differ from a plain program's by a relative error of at most 0.017.
Values may be sent and summed in bfloat16 or wider, within the bound.
A program may use at most 64 MiB of HBM per device.

v0:
```python
import math

import jax
import jax.numpy as jnp
from jax import lax
from jax.sharding import PartitionSpec as P

HEAD_DIM = 128


def shifted(value, axis, by):
    count = lax.axis_size(axis)
    return lax.ppermute(value, axis, [(i, (i + by) % count) for i in range(count)])


def half_grads(queries, grads_out, key_stack, value_stack, place, span):
    token_count = queries.shape[0]
    heads = queries.shape[1]
    share = queries.shape[2]
    score_scale = 1.0 / math.sqrt(queries.shape[3])
    row_index = lax.broadcasted_iota(jnp.int32, (token_count, token_count), 0)
    col_index = lax.broadcasted_iota(jnp.int32, (token_count, token_count), 1)
    causal = col_index <= row_index
    blocks = jnp.arange(span, dtype=jnp.int32)

    def masked_scores(block, keys):
        scores = (
            jnp.einsum("thqd,lhd->hqtl", queries, keys, preferred_element_type=jnp.float32)
            * score_scale
        )
        return jnp.where(jnp.logical_or(block > 0, causal), scores, -jnp.inf)

    def seen_by(block):
        return jnp.logical_or(block == 0, place >= block)

    def first_pass(carry, items):
        block, keys, values = items

        def first_update(state):
            top, total, accum = state
            masked = masked_scores(block, keys)
            dweights = jnp.einsum(
                "thqd,lhd->hqtl", grads_out, values, preferred_element_type=jnp.float32
            )
            new_top = jnp.maximum(top, jnp.max(masked, axis=-1, keepdims=True))
            factor = jnp.exp(top - new_top)
            raised = jnp.exp(masked - new_top)
            return (
                new_top,
                total * factor + jnp.sum(raised, axis=-1, keepdims=True),
                accum * factor + jnp.sum(raised * dweights, axis=-1, keepdims=True),
            )

        return (lax.cond(seen_by(block), first_update, lambda state: state, carry), None)

    start = (
        jnp.full((heads, share, token_count, 1), -jnp.inf, jnp.float32),
        jnp.zeros((heads, share, token_count, 1), jnp.float32),
        jnp.zeros((heads, share, token_count, 1), jnp.float32),
    )
    (top, total, accum), _ = lax.scan(first_pass, start, (blocks, key_stack, value_stack))
    lse = top + jnp.log(total)
    row_delta = accum / total

    def second_pass(grad_q, items):
        block, keys, values = items

        def second_update(current):
            weights = jnp.exp(masked_scores(block, keys) - lse)
            dweights = jnp.einsum(
                "thqd,lhd->hqtl", grads_out, values, preferred_element_type=jnp.float32
            )
            dscores = (weights * (dweights - row_delta)).astype(jnp.bfloat16)
            weights_low = weights.astype(jnp.bfloat16)
            grad_v = jnp.einsum(
                "hqtl,thqd->lhd", weights_low, grads_out, preferred_element_type=jnp.float32
            )
            grad_k = (
                jnp.einsum("hqtl,thqd->lhd", dscores, queries, preferred_element_type=jnp.float32)
                * score_scale
            )
            grad_step = (
                jnp.einsum("hqtl,lhd->thqd", dscores, keys, preferred_element_type=jnp.float32)
                * score_scale
            )
            return (current + grad_step, grad_k, grad_v)

        def skip(current):
            empty = jnp.zeros((token_count, heads, queries.shape[3]), jnp.float32)
            return (current, empty, empty)

        new_q, grad_k, grad_v = lax.cond(seen_by(block), second_update, skip, grad_q)
        return (new_q, (grad_k, grad_v))

    grad_q, (key_grads, value_grads) = lax.scan(
        second_pass, jnp.zeros(queries.shape, jnp.float32), (blocks, key_stack, value_stack)
    )
    return (grad_q, key_grads, value_grads)


def adapter_contribution(hidden_inputs, grads):
    return lax.dot_general(
        hidden_inputs, grads, (((0,), (0,)), ((), ())), preferred_element_type=jnp.float32
    )


def on_device(
    all_query_heads,
    grouped_key_heads,
    grouped_value_heads,
    output_gradient,
    head_ordering,
    adapter_activations,
):
    token_count = all_query_heads.shape[1]
    ordering = head_ordering[0]
    kv_heads = ordering.shape[0]
    half_heads = kv_heads // 2
    share = all_query_heads.shape[2] // (kv_heads * HEAD_DIM)
    queries = jnp.take(
        all_query_heads.reshape(token_count, kv_heads, share, HEAD_DIM), ordering, axis=1
    )
    grads_out = jnp.take(
        output_gradient.reshape(token_count, kv_heads, share, HEAD_DIM), ordering, axis=1
    )
    keys = jnp.take(grouped_key_heads.reshape(token_count, kv_heads, HEAD_DIM), ordering, axis=1)
    values = jnp.take(
        grouped_value_heads.reshape(token_count, kv_heads, HEAD_DIM), ordering, axis=1
    )
    span = min(16, lax.axis_size("ctx"))
    device_index = lax.axis_index("ctx")
    plain_place = device_index % span
    shifted_place = (device_index + span // 2) % span

    def pass_on(carry, unused):
        moved = shifted((carry[0], carry[1]), "ctx", 1)
        return (moved, moved)

    _, (got_keys, got_values) = lax.scan(pass_on, (keys, values), None, length=span - 1)
    key_stack = jnp.concatenate([keys[None], got_keys], axis=0)
    value_stack = jnp.concatenate([values[None], got_values], axis=0)
    shift_q, shift_k, shift_v = half_grads(
        queries[:, :half_heads],
        grads_out[:, :half_heads],
        key_stack[:, :, :half_heads],
        value_stack[:, :, :half_heads],
        shifted_place,
        span,
    )
    plain_q, plain_k, plain_v = half_grads(
        queries[:, half_heads:],
        grads_out[:, half_heads:],
        key_stack[:, :, half_heads:],
        value_stack[:, :, half_heads:],
        plain_place,
        span,
    )
    key_grads = jnp.concatenate([shift_k, plain_k], axis=2)
    value_grads = jnp.concatenate([shift_v, plain_v], axis=2)

    def pass_back(carry, items):
        moved = (
            shifted((carry[0] + items[0]).astype(jnp.bfloat16), "ctx", -1).astype(jnp.float32),
            shifted((carry[1] + items[1]).astype(jnp.bfloat16), "ctx", -1).astype(jnp.float32),
        )
        return (moved, None)

    empty = jnp.zeros(key_grads.shape[1:], jnp.float32)
    (back_keys, back_values), _ = lax.scan(
        pass_back, (empty, empty), (key_grads[1:], value_grads[1:]), reverse=True
    )
    own_keys = key_grads[0] + back_keys
    own_values = value_grads[0] + back_values
    low_q = jnp.concatenate([shift_q, plain_q], axis=1).astype(jnp.bfloat16)
    low_k = own_keys.astype(jnp.bfloat16)
    low_v = own_values.astype(jnp.bfloat16)
    positions = jnp.arange(kv_heads, dtype=jnp.int32)
    inverse = jnp.sum(
        positions[:, None] * (ordering[:, None] == positions[None, :]).astype(jnp.int32), axis=0
    )
    flattened_query = jnp.take(low_q, inverse, axis=1).reshape(token_count, -1)
    flattened_key = jnp.take(low_k, inverse, axis=1).reshape(token_count, -1)
    flattened_value = jnp.take(low_v, inverse, axis=1).reshape(token_count, -1)
    adapter_rank_size = adapter_activations.shape[2] // 3
    hidden_inputs = adapter_activations.reshape(token_count, 3 * adapter_rank_size)
    query_contribution = adapter_contribution(hidden_inputs[:, :adapter_rank_size], flattened_query)
    term_pairs = jnp.concatenate(
        [
            adapter_contribution(
                hidden_inputs[:, adapter_rank_size : 2 * adapter_rank_size], flattened_key
            ),
            adapter_contribution(hidden_inputs[:, 2 * adapter_rank_size :], flattened_value),
        ],
        axis=1,
    )
    adapter_query, adapter_pairings = (
        lax.psum_scatter(query_contribution, ("ctx", "dp"), scatter_dimension=1, tiled=True),
        lax.psum_scatter(term_pairs, ("ctx", "dp"), scatter_dimension=1, tiled=True),
    )
    return (
        flattened_query.reshape(1, token_count, -1),
        flattened_key.reshape(1, token_count, -1),
        flattened_value.reshape(1, token_count, -1),
        adapter_query,
        adapter_pairings,
    )


def solution(mesh):
    placed = (
        P("dp", "ctx", None),
        P("dp", "ctx", None),
        P("dp", "ctx", None),
        P("dp", "ctx", None),
        P("dp", None),
        P("dp", "ctx", None),
    )
    return jax.shard_map(
        on_device,
        mesh=mesh,
        in_specs=placed,
        out_specs=(
            P("dp", "ctx", None),
            P("dp", "ctx", None),
            P("dp", "ctx", None),
            P(None, ("ctx", "dp")),
            P(None, ("ctx", "dp")),
        ),
        check_vma=False,
    )
```

profile of v0, /device:TPU:1, one launch (start us, length us, event | category | flops | bytes accessed | tf_op | source)
XLA Modules:
  0.0 2281.6 jit_solution(7619087305095121283)
XLA Ops:
  20.7 172.2 %while.99 = (s32[]{:T(128)}, bf16[128,4,128]{2,1,0:T(4,128)(2,1)S(1)}, bf16[128,4,128]{2,1,0:T(4,128)(2,1)S(1)}, bf16[15,128,4,128]{3,1,2,0:T(8,128)(2,1)}, bf16[15,128,4,128]{3,1,2,0:T(8,128)(2,1)}, /*index=5*/s32[]{:T(128)}) while((s32[]{:T(128)}, bf16[128,4,128]{2,1,0:T(4,128)(2,1)S(1)}, bf16[128,4,128]{2,1,0:T(4,128)(2,1)S(1)}, ...), condition=%wide.region_1.3_spmd, body=%wide.region_0.0_spmd.sunk | while | flops 2 | bytes 2097317 | solution.py:139
  25.1 8.9 collective-permute-done
  37.8 7.9 collective-permute-done
  49.4 7.9 collective-permute-done
  60.2 7.9 collective-permute-done
  70.5 7.9 collective-permute-done
  80.8 7.9 collective-permute-done
  91.1 7.9 collective-permute-done
  101.4 7.9 collective-permute-done
  111.7 8.6 collective-permute-done
  122.6 9.6 collective-permute-done
  134.7 9.6 collective-permute-done
  148.0 8.7 collective-permute-done
  160.6 7.9 collective-permute-done
  172.2 7.9 collective-permute-done
  182.9 7.9 collective-permute-done
  197.3 34.6 %while.102 = (s32[]{:T(128)}, f32[2,8,128,1]{2,1,0,3:T(8,128)S(1)}, f32[2,8,128,1]{2,1,0,3:T(8,128)S(1)}, f32[2,8,128,1]{2,1,0,3:T(8,128)S(1)}, s32[16]{0:T(128)...) while((s32[]{:T(128)}, f32[2,8,128,1]{2,1,0,3:T(8,128)S(1)}, ...), condition=%wide.region_19.22_spmd.clone, body=%wide.region_13.21_spmd.clone.sunk | while | flops 136353792 | bytes 4769085 | solution.py:61
  235.8 56.3 %while.103 = (s32[]{:T(128)}, f32[128,2,8,128]{3,0,2,1:T(8,128)S(1)}, f32[16,128,2,128]{3,1,2,0:T(8,128)}, f32[16,128,2,128]{3,1,2,0:T(8,128)}, s32[16]{0:T(128)...) while((s32[]{:T(128)}, ...), condition=%wide.region_23.26_spmd.clone, body=%wide.region_20.25_spmd.clone.sunk | while | flops 337969152 | bytes 10209581 | solution.py:95
  294.5 52.6 %while.100 = (s32[]{:T(128)}, f32[2,8,128,1]{2,1,0,3:T(8,128)S(1)}, f32[2,8,128,1]{2,1,0,3:T(8,128)S(1)}, f32[2,8,128,1]{2,1,0,3:T(8,128)S(1)}, s32[16]{0:T(128)...) while((s32[]{:T(128)}, f32[2,8,128,1]{2,1,0,3:T(8,128)S(1)}, ...), condition=%wide.region_8.11_spmd.clone, body=%wide.region_2.10_spmd.clone.sunk | while | flops 136353792 | bytes 4768577 | solution.py:61
  351.3 97.4 %while.101 = (s32[]{:T(128)}, f32[128,2,8,128]{3,0,2,1:T(8,128)S(1)}, f32[16,128,2,128]{3,1,2,0:T(8,128)}, f32[16,128,2,128]{3,1,2,0:T(8,128)}, s32[16]{0:T(128)...) while((s32[]{:T(128)}, ...), condition=%wide.region_12.15_spmd.clone, body=%wide.region_9.14_spmd.clone.sunk | while | flops 337969152 | bytes 10209581 | solution.py:95
  459.4 277.6 %while.104 = (s32[]{:T(128)}, f32[128,4,128]{2,1,0:T(4,128)S(1)}, f32[128,4,128]{2,1,0:T(4,128)S(1)}, f32[15,128,4,128]{3,1,2,0:T(8,128)}, f32[15,128,4,128]{3,1...) while((s32[]{:T(128)}, f32[128,4,128]{2,1,0:T(4,128)S(1)}, f32[128,4,128]{2,1,0:T(4,128)S(1)}, ...), condition=%wide.region_26.29_spmd.clone, body=%wide.region_25.28_spmd.clone.sunk | while | flops 524292 | bytes 4194500 | solution.py:169
  460.6 112.4 %collective-permute-start.2 = (bf16[128,4,128]{2,1,0:T(4,128)(2,1)S(1)}, bf16[128,4,128]{2,1,0:T(4,128)(2,1)S(1)}, u32[]{:S(2)}, u32[]{:S(2)}) collective-permute-start(bf16[128,4,128]{2,1,0:T(4,128)(2,1)S(1)} %fusion.116), channel_id=1, source_target_pairs={{0,252},{4,0},{8,4},{12,8},{16,12},{20,16},{24,20},{28,24},{32,28}... | collective-permute-start | bytes 393224 | tf_op jit(solution)/shard_map/while/body/eval_jaxpr/ppermute | solution.py:13
  750.6 257.8 %all-reduce.3.cloned.1.call-done = f32[16,1024]{1,0:T(8,128)} async-done(((f32[16,1024]{1,0:T(8,128)}), f32[16,1024]{1,0:T(8,128)}) %all-reduce.3.cloned.1.call-update) | async-done | bytes 65552
  1009.8 1263.6 %reduce-scatter.5.cloned.1.call-done = f32[16,16]{1,0:T(8,128)} async-done(((f32[4096,16]{1,0:T(8,128)}), f32[16,16]{1,0:T(8,128)}) %reduce-scatter.5.cloned.1.call-update) | async-done | bytes 1040
  (828 shorter events, 484.5 us)
Async XLA Ops:
  7.2 1001.2 %all-reduce.3.cloned.1.call-start = ((), (), s32[]{:S(2)}) async-start(), calls=%async_computation.2 | async-start | bytes 131072
  20.9 13.1 collective-permute-start
  23.5 13.3 collective-permute-start.1
  37.7 10.8 collective-permute-start.1
  49.4 9.9 collective-permute-start.1
  60.1 9.4 collective-permute-start.1
  70.4 9.4 collective-permute-start.1
  80.7 9.4 collective-permute-start.1
  91.0 9.4 collective-permute-start.1
  101.3 9.4 collective-permute-start.1
  111.5 8.7 collective-permute-start
  111.6 10.1 collective-permute-start.1
  122.5 9.8 collective-permute-start
  122.6 11.2 collective-permute-start.1
  134.5 9.8 collective-permute-start
  134.6 12.5 collective-permute-start.1
  147.9 8.9 collective-permute-start
  147.9 11.6 collective-permute-start.1
  160.5 10.7 collective-permute-start.1
  172.1 9.8 collective-permute-start.1
  182.8 9.4 collective-permute-start.1
  460.6 114.4 %collective-permute-start.2 = (bf16[128,4,128]{2,1,0:T(4,128)(2,1)S(1)}, bf16[128,4,128]{2,1,0:T(4,128)(2,1)S(1)}, u32[]{:S(2)}, u32[]{:S(2)}) collective-permute-start(bf16[128,4,128]{2,1,0:T(4,128)(2,1)S(1)} %fusion.116), channel_id=1, source_target_pairs={{0,252},{4,0},{8,4},{12,8},{16,12},{20,16},{24,20},{28,24},{32,28}... | collective-permute-start | bytes 393224 | tf_op jit(solution)/shard_map/while/body/eval_jaxpr/ppermute | solution.py:13
  633.3 8.8 collective-permute-start.2
  741.8 1531.6 %reduce-scatter.5.cloned.1.call-start = ((), (), s32[]{:S(2)}) async-start(), calls=%async_computation.1 | async-start | bytes 2105344
  (52 other events, 723.4 us)
Sparse Core Ops, SparseCore 0:
  741.9 266.3 all-reduce.2
  1010.9 1262.5 reduce-scatter.4
where the time goes:
time: 2290 us; the launch traced here: 2280 us
  waiting for transfers between devices  1720 us (75%)
  starting transfers between devices  188 us (8%)
  local copies, waits for them, and re-layouts  177 us (8%)
  loops' own time  98.9 us (4%)
  matrix products  57.8 us (3%)
    unnamed x4, waiting for transfers between devices  1520 us
    ppermute x60, waiting for transfers between devices, shifted(): lax.ppermute(value, axis, [(i, (i + by) % count) for i in range(count)])  203 us
    ppermute x60, starting transfers between devices, shifted(): lax.ppermute(value, axis, [(i, (i + by) % count) for i in range(count)])  187 us
    dynamic_slice x64, local copies, waits for them, and re-layouts, half_grads(): lax.scan(first_pass, start, (blocks, key_stack, value_stack))  59.5 us
  transfers between devices with their start and end apart: 62, of which 62 were waited for; matrix products, arithmetic and copies ran while one was open for 2% of the time, Pallas kernels for 0%

commit v1 on v0

v1 whole, which is shorter than its diff:
```python
import math

import jax
import jax.numpy as jnp
from jax import lax
from jax.experimental import pallas as pl
from jax.experimental.pallas import tpu as pltpu
from jax.sharding import PartitionSpec as P

MESH = pl.DeviceIdType.MESH
F32 = jnp.float32
BF16 = jnp.bfloat16
BLOCK = 128
KV_HEADS = 4
SHARE = 8
ROWS = SHARE * BLOCK
LINE = 8
RANK = 16
SCALE = 1.0 / math.sqrt(BLOCK)
EXP2_SCALE = SCALE / math.log(2.0)
HIDDEN = -1e30


def dot(a, b, a_dim, b_dim):
    return lax.dot_general(a, b, (((a_dim,), (b_dim,)), ((), ())), preferred_element_type=F32)


def kernel(
    order_ref,
    q_ref,
    k_ref,
    v_ref,
    g_ref,
    act_ref,
    dq_ref,
    dk_ref,
    dv_ref,
    aq_ref,
    akv_ref,
    own_kv,
    line_kv,
    prev_kv,
    qs,
    gs,
    top,
    total,
    accum,
    p_low,
    s_low,
    dq_t,
    part,
    prev_part,
    next_part,
    left_out,
    left_in,
    right_out,
    right_in,
    final,
    terms,
    stage1,
    terms2,
    stage2,
    terms3,
    stage3,
    load_sem,
    g_right_e,
    g_right_l,
    g_left_e,
    g_left_l,
    g_next,
    b_prev,
    b_left_e,
    b_left_l,
    b_right_e,
    b_right_l,
    a_sem1,
    a_sem2,
    a_sem3,
):
    ctx = lax.axis_index("ctx")
    dp = lax.axis_index("dp")
    z = lax.rem(ctx, LINE)
    line = ctx // LINE
    base = line * LINE
    left = base + lax.rem(z + LINE - 1, LINE)
    right = base + lax.rem(z + 1, LINE)
    after = lax.rem(line + 1, LINE) * LINE + z
    before = lax.rem(line + LINE - 1, LINE) * LINE + z

    def copy(src, dst, sems, index, target):
        return pltpu.make_async_remote_copy(
            src_ref=src,
            dst_ref=dst,
            send_sem=sems.at[0, index],
            recv_sem=sems.at[1, index],
            device_id=target,
            device_id_type=MESH,
        )

    def slot(by):
        return lax.rem(z + by + LINE, LINE)

    def right_e(s, block):
        view = line_kv.at[block, pl.ds(0, 4)]
        return copy(view, view, g_right_e, s - 1, {"ctx": right})

    def right_l(s, block):
        view = line_kv.at[block, pl.ds(4, 4)]
        return copy(view, view, g_right_l, s - 1, {"ctx": right})

    def left_e(s, block):
        view = line_kv.at[block, pl.ds(0, 4)]
        return copy(view, view, g_left_e, s - 1, {"ctx": left})

    def left_l(s, block):
        view = line_kv.at[block, pl.ds(4, 4)]
        return copy(view, view, g_left_l, s - 1, {"ctx": left})

    def to_next(index, block):
        return copy(
            line_kv.at[block, pl.ds(0, 4)], prev_kv.at[block], g_next, index, {"ctx": after}
        )

    def to_prev(index):
        return copy(prev_part.at[index], next_part.at[index], b_prev, index, {"ctx": before})

    def back_left(s, first, sems):
        return copy(
            left_out.at[s - 1, pl.ds(first, 4)],
            left_in.at[s - 1, pl.ds(first, 4)],
            sems,
            s - 1,
            {"ctx": left},
        )

    def back_right(s, first, sems):
        return copy(
            right_out.at[s - 1, pl.ds(first, 4)],
            right_in.at[s - 1, pl.ds(first, 4)],
            sems,
            s - 1,
            {"ctx": right},
        )

    def load(src, dst, row, h, r):
        return pltpu.make_async_copy(
            src.at[:, pl.ds((h * SHARE + r) * BLOCK, BLOCK)],
            dst.at[h, pl.ds(r * BLOCK, BLOCK), :],
            load_sem.at[row, h * SHARE + r],
        )

    for h in range(KV_HEADS):
        for r in range(SHARE):
            load(q_ref, qs, 0, h, r).start()
            load(g_ref, gs, 1, h, r).start()

    barrier = pltpu.get_barrier_semaphore()
    for by in range(1, LINE):
        pl.semaphore_signal(barrier, inc=1, device_id={"ctx": base + slot(by)}, device_id_type=MESH)
        pl.semaphore_signal(
            barrier,
            inc=1,
            device_id={"ctx": lax.rem(line + by, LINE) * LINE + z},
            device_id_type=MESH,
        )
    for by in range(1, 4):
        pl.semaphore_signal(
            barrier, inc=1, device_id={"dp": lax.rem(dp + by, 4)}, device_id_type=MESH
        )
    pl.semaphore_wait(barrier, 2 * (LINE - 1) + 3)

    swap = 2 * (1 - lax.rem(line, 2))
    ordering = [order_ref[0, lax.rem(j + swap, KV_HEADS)] for j in range(KV_HEADS)]
    places = []
    for h in range(KV_HEADS):
        place = jnp.int32(0)
        for j in range(1, KV_HEADS):
            place = jnp.maximum(place, jnp.where(ordering[j] == h, j, 0))
        places.append(place)

    for h in range(KV_HEADS):
        own_kv[h, 0] = k_ref[:, pl.ds(h * BLOCK, BLOCK)]
        own_kv[h, 1] = v_ref[:, pl.ds(h * BLOCK, BLOCK)]
    for j in range(KV_HEADS):
        line_kv[z, 2 * j] = own_kv[ordering[j], 0]
        line_kv[z, 2 * j + 1] = own_kv[ordering[j], 1]

    right_e(1, z).start()
    left_e(1, z).start()
    to_next(0, z).start()

    @pl.when(z < LINE - 1)
    def _():
        right_l(1, z).start()

    @pl.when(z <= 2)
    def _():
        left_l(1, z).start()

    top[...] = jnp.full(top.shape, HIDDEN, F32)
    total[...] = jnp.zeros(total.shape, F32)
    accum[...] = jnp.zeros(accum.shape, F32)
    dq_t[...] = jnp.zeros(dq_t.shape, F32)

    width = 2 * BLOCK

    def name(j):
        return order_ref[0, lax.rem(j + swap, KV_HEADS)]

    def scores(j, piece, keys, diagonal):
        q = qs[name(j), pl.ds(piece * width, width), :]
        s = dot(keys, q, 1, 1) * EXP2_SCALE
        if diagonal:
            key_at = lax.broadcasted_iota(jnp.int32, (BLOCK, width), 0)
            query_at = lax.rem(lax.broadcasted_iota(jnp.int32, (BLOCK, width), 1), BLOCK)
            own = jnp.where(key_at <= query_at, s[-BLOCK:], HIDDEN)
            s = own if s.shape[0] == BLOCK else jnp.concatenate([s[:-BLOCK], own], axis=0)
        return s

    def first_pass(j, keys, values, diagonal):
        for piece in range(ROWS // width):
            cols = pl.ds(piece * width, width)
            s = scores(j, piece, keys, diagonal)
            old = top[j, :, cols]
            new = jnp.maximum(old, jnp.max(s, axis=0, keepdims=True))
            e = jnp.exp2(s - new)
            dp_ = dot(values, gs[name(j), cols, :], 1, 1)
            factor = jnp.exp2(old - new)
            total[j, :, cols] = total[j, :, cols] * factor + jnp.sum(e, axis=0, keepdims=True)
            accum[j, :, cols] = accum[j, :, cols] * factor + jnp.sum(e * dp_, axis=0, keepdims=True)
            top[j, :, cols] = new

    def second_pass(j, keys, values, diagonal):
        count = keys.shape[0]
        for piece in range(ROWS // width):
            cols = pl.ds(piece * width, width)
            p = jnp.exp2(scores(j, piece, keys, diagonal) - top[j, :, cols])
            dp_ = dot(values, gs[name(j), cols, :], 1, 1)
            s_low[pl.ds(0, count), cols] = (p * (dp_ - accum[j, :, cols])).astype(BF16)
            p_low[pl.ds(0, count), cols] = p.astype(BF16)
        ds = s_low[pl.ds(0, count), :]
        dk = dot(ds, qs[name(j)], 1, 0)
        dv = dot(p_low[pl.ds(0, count), :], gs[name(j)], 1, 0)
        dq_t[j] += dot(keys, ds, 0, 0)
        return dk, dv

    def own_keys(j, blocks):
        keys = [line_kv[b, 2 * j] for b in blocks]
        values = [line_kv[b, 2 * j + 1] for b in blocks]
        if len(blocks) == 1:
            return keys[0], values[0]
        return jnp.concatenate(keys, axis=0), jnp.concatenate(values, axis=0)

    def prev_keys(j, blocks):
        keys = [prev_kv[b, 2 * j] for b in blocks]
        values = [prev_kv[b, 2 * j + 1] for b in blocks]
        return jnp.concatenate(keys, axis=0), jnp.concatenate(values, axis=0)

    def own_cases(t, run):
        far = 9 - t

        @pl.when((t == 1) & (z >= 1))
        def _():
            run((1, 0), True)

        @pl.when((t == 1) & (z == 0))
        def _():
            run((0,), True)

        @pl.when((t > 1) & (z >= far))
        def _():
            run((t, far), False)

        @pl.when((t > 1) & (z >= t) & (z < far))
        def _():
            run((t,), False)

    def prev_pair(t):
        second = jnp.where(t == 1, 0, 2 * t - 2)
        return (2 * t - 1, second), (slot(-t), lax.rem(z + t - 1, LINE))

    def gather_step(t, carry):
        block = slot(-t)
        right_e(t, block).wait_recv()

        @pl.when(t < 4)
        def _():
            right_e(t + 1, block).start()

        to_next(2 * t - 1, block).start()

        @pl.when(t < 4)
        def _():
            other = slot(t)
            left_e(t, other).wait_recv()

            @pl.when(t < 3)
            def _():
                left_e(t + 1, other).start()

            to_next(2 * t, other).start()

            @pl.when(other <= 2)
            def _():
                left_l(t, other).wait_recv()

                @pl.when(t < 3)
                def _():
                    left_l(t + 1, other).start()

        @pl.when(z >= t)
        def _():
            right_l(t, block).wait_recv()

            @pl.when((t < 4) & (z < LINE - 1))
            def _():
                right_l(t + 1, block).start()

        def run(distances, diagonal):
            blocks = [slot(-d) for d in distances]

            def head(j, c):
                keys, values = own_keys(j, blocks)
                first_pass(j, keys, values, diagonal)
                return c

            lax.fori_loop(0, KV_HEADS, head, 0)

        own_cases(t, run)
        indices, blocks = prev_pair(t)
        for index, b in zip(indices, blocks):
            to_next(index, b).wait_recv()

        def head(j, c):
            keys, values = prev_keys(j, blocks)
            first_pass(j + 2, keys, values, False)
            return c

        lax.fori_loop(0, 2, head, 0)
        return carry

    for h in range(KV_HEADS):
        for r in range(SHARE):
            load(q_ref, qs, 0, h, r).wait()
            load(g_ref, gs, 1, h, r).wait()
    lax.fori_loop(1, 5, gather_step, 0)

    top[...] = top[...] + jnp.log2(total[...])
    accum[...] = accum[...] / total[...]

    def prev_step(t):
        indices, blocks = prev_pair(t)

        def head(j, c):
            keys, values = prev_keys(j, blocks)
            dk, dv = second_pass(j + 2, keys, values, False)
            for i, index in enumerate(indices):
                rows = slice(i * BLOCK, (i + 1) * BLOCK)
                prev_part[index, 2 * j] = dk[rows].astype(BF16)
                prev_part[index, 2 * j + 1] = dv[rows].astype(BF16)
            return c

        lax.fori_loop(0, 2, head, 0)
        for index in indices:
            to_prev(index).start()

    def own_step(t):
        far = jnp.where(t == 1, 0, 9 - t)

        @pl.when(z < far)
        def _():
            part[far] = jnp.zeros(part.shape[1:], F32)

        @pl.when(z < t)
        def _():
            part[t] = jnp.zeros(part.shape[1:], F32)

        def run(distances, diagonal):
            blocks = [slot(-d) for d in distances]

            def head(j, c):
                keys, values = own_keys(j, blocks)
                dk, dv = second_pass(j, keys, values, diagonal)
                for i, d in enumerate(distances):
                    rows = slice(i * BLOCK, (i + 1) * BLOCK)
                    part[d, 2 * j] = dk[rows]
                    part[d, 2 * j + 1] = dv[rows]
                return c

            lax.fori_loop(0, KV_HEADS, head, 0)

        own_cases(t, run)

    early, late = pl.ds(0, 4), pl.ds(4, 4)

    def flush(t):
        @pl.when(t < 4)
        def _():
            back_left(t + 1, 0, b_left_e).wait_recv()
            part[t, early] += left_in[t, early].astype(F32)

        to_prev(2 * t - 1).wait_recv()
        left_out[t - 1, early] = (part[t, early] + next_part[2 * t - 1].astype(F32)).astype(BF16)
        back_left(t, 0, b_left_e).start()

        @pl.when(z >= t)
        def _():
            @pl.when((t < 4) & (z < LINE - 1))
            def _():
                back_left(t + 1, 4, b_left_l).wait_recv()
                part[t, late] += left_in[t, late].astype(F32)

            left_out[t - 1, late] = part[t, late].astype(BF16)
            back_left(t, 4, b_left_l).start()

        @pl.when(t > 1)
        def _():
            s = t - 1
            far = 9 - t

            @pl.when(t < 4)
            def _():
                back_right(s + 1, 0, b_right_e).wait_recv()
                part[far, early] += right_in[s, early].astype(F32)

            to_prev(2 * s).wait_recv()
            right_out[s - 1, early] = (part[far, early] + next_part[2 * s].astype(F32)).astype(BF16)
            back_right(s, 0, b_right_e).start()

            @pl.when(slot(s) <= 2)
            def _():
                @pl.when(t < 4)
                def _():
                    back_right(s + 1, 4, b_right_l).wait_recv()
                    part[far, late] += right_in[s, late].astype(F32)

                right_out[s - 1, late] = part[far, late].astype(BF16)
                back_right(s, 4, b_right_l).start()

    prev_step(4)

    def back_step(i, carry):
        t = 4 - i

        @pl.when(t > 1)
        def _():
            prev_step(t - 1)

        own_step(t)
        flush(t)
        return carry

    lax.fori_loop(0, 4, back_step, 0)

    for h in range(KV_HEADS):
        for r in range(SHARE):
            block = dq_t[places[h], :, pl.ds(r * BLOCK, BLOCK)] * SCALE
            dq_ref[:, pl.ds((h * SHARE + r) * BLOCK, BLOCK)] = block.astype(BF16).T
    for c in range(LINE):
        terms[c, :, pl.ds(0, 512)] = dot(
            act_ref[:, 0:RANK], dq_ref[:, pl.ds(c * 512, 512)], 0, 0
        )

    to_prev(0).wait_recv()
    back_left(1, 0, b_left_e).wait_recv()
    back_right(1, 0, b_right_e).wait_recv()
    final[early] = (
        part[0, early]
        + next_part[0].astype(F32)
        + left_in[0, early].astype(F32)
        + right_in[0, early].astype(F32)
    )
    final[late] = part[0, late]

    @pl.when(z < LINE - 1)
    def _():
        back_left(1, 4, b_left_l).wait_recv()
        final[late] += left_in[0, late].astype(F32)

    @pl.when(z <= 2)
    def _():
        back_right(1, 4, b_right_l).wait_recv()
        final[late] += right_in[0, late].astype(F32)

    for h in range(KV_HEADS):
        columns = pl.ds(h * BLOCK, BLOCK)
        dk_ref[:, columns] = (final[2 * places[h]] * SCALE).astype(BF16)
        dv_ref[:, columns] = final[2 * places[h] + 1].astype(BF16)
    for h in range(KV_HEADS):
        columns = pl.ds(h * BLOCK, BLOCK)
        terms[h, :, pl.ds(512, BLOCK)] = dot(
            act_ref[:, RANK : 2 * RANK], dk_ref[:, columns], 0, 0
        )
        terms[KV_HEADS + h, :, pl.ds(512, BLOCK)] = dot(
            act_ref[:, 2 * RANK : 3 * RANK], dv_ref[:, columns], 0, 0
        )

    def stage1_copy(by):
        other = lax.rem(line + by, LINE)
        return copy(
            terms.at[other], stage1.at[by - 1], a_sem1, by - 1, {"ctx": other * LINE + z}
        )

    def stage2_copy(by):
        other = slot(by)
        return copy(
            terms2.at[other // 2], stage2.at[by - 1], a_sem2, by - 1, {"ctx": base + other}
        )

    def stage3_copy(by):
        return copy(terms3, stage3.at[by - 1], a_sem3, by - 1, {"dp": lax.rem(dp + by, 4)})

    for by in range(1, LINE):
        stage1_copy(by).start()
    value = terms[line]
    for by in range(1, LINE):
        stage1_copy(by).wait_recv()
        value = value + stage1[by - 1]
    for c in range(4):
        terms2[c, :, pl.ds(0, BLOCK)] = value[:, c * BLOCK : (c + 1) * BLOCK]
        terms2[c, :, pl.ds(BLOCK, BLOCK)] = value[:, 4 * BLOCK :]
    for by in range(1, LINE):
        stage2_copy(by).start()
    value = terms2[z // 2]
    for by in range(1, LINE):
        stage2_copy(by).wait_recv()
        value = value + stage2[by - 1]
    terms3[...] = value
    for by in range(1, 4):
        stage3_copy(by).start()
    for by in range(1, 4):
        stage3_copy(by).wait_recv()
        value = value + stage3[by - 1]
    q_first = lax.rem(z, 2) * 64 + dp * 16
    kv_first = z * 16 + dp * 4
    aq_ref[...] = pltpu.roll(value[:, :BLOCK], lax.rem(BLOCK - q_first, BLOCK), 1)[:, :16]
    akv_ref[...] = pltpu.roll(value[:, BLOCK:], lax.rem(BLOCK - kv_first, BLOCK), 1)[:, :4]

    for s in range(1, 5):
        block = slot(1 - s)
        right_e(s, block).wait_send()
        back_left(s, 0, b_left_e).wait_send()

        @pl.when((z >= s - 1) & (z < LINE - 1))
        def _():
            right_l(s, block).wait_send()

        @pl.when(z >= s)
        def _():
            back_left(s, 4, b_left_l).wait_send()

    for s in range(1, 4):
        block = slot(s - 1)
        left_e(s, block).wait_send()
        back_right(s, 0, b_right_e).wait_send()

        @pl.when(block <= 2)
        def _():
            left_l(s, block).wait_send()

        @pl.when(slot(s) <= 2)
        def _():
            back_right(s, 4, b_right_l).wait_send()

    for index in range(LINE):
        to_next(index, z).wait_send()
        to_prev(index).wait_send()
    for by in range(1, LINE):
        stage1_copy(by).wait_send()
        stage2_copy(by).wait_send()
    for by in range(1, 4):
        stage3_copy(by).wait_send()


def on_device(queries, keys, values, grads_out, ordering, activations):
    count = queries.shape[1]
    vmem = pl.BlockSpec(memory_space=pltpu.VMEM)
    hbm = pl.BlockSpec(memory_space=pl.ANY)
    pair = (2 * KV_HEADS, BLOCK, BLOCK)
    half = (KV_HEADS, BLOCK, BLOCK)

    def sems(n):
        return pltpu.SemaphoreType.DMA((2, n))

    dq, dk, dv, aq, akv = pl.pallas_call(
        kernel,
        out_shape=(
            jax.ShapeDtypeStruct((count, queries.shape[2]), BF16),
            jax.ShapeDtypeStruct((count, keys.shape[2]), BF16),
            jax.ShapeDtypeStruct((count, values.shape[2]), BF16),
            jax.ShapeDtypeStruct((RANK, 16), F32),
            jax.ShapeDtypeStruct((RANK, 4), F32),
        ),
        in_specs=[pl.BlockSpec(memory_space=pltpu.SMEM), hbm, vmem, vmem, hbm, vmem],
        out_specs=(vmem,) * 5,
        scratch_shapes=[
            pltpu.VMEM((KV_HEADS, 2, BLOCK, BLOCK), BF16),
            pltpu.VMEM((LINE,) + pair, BF16),
            pltpu.VMEM((LINE,) + half, BF16),
            pltpu.VMEM((KV_HEADS, ROWS, BLOCK), BF16),
            pltpu.VMEM((KV_HEADS, ROWS, BLOCK), BF16),
            pltpu.VMEM((KV_HEADS, 1, ROWS), F32),
            pltpu.VMEM((KV_HEADS, 1, ROWS), F32),
            pltpu.VMEM((KV_HEADS, 1, ROWS), F32),
            pltpu.VMEM((2 * BLOCK, ROWS), BF16),
            pltpu.VMEM((2 * BLOCK, ROWS), BF16),
            pltpu.VMEM((KV_HEADS, BLOCK, ROWS), F32),
            pltpu.VMEM((LINE,) + pair, F32),
            pltpu.VMEM((LINE,) + half, BF16),
            pltpu.VMEM((LINE,) + half, BF16),
            pltpu.VMEM((4,) + pair, BF16),
            pltpu.VMEM((4,) + pair, BF16),
            pltpu.VMEM((3,) + pair, BF16),
            pltpu.VMEM((3,) + pair, BF16),
            pltpu.VMEM(pair, F32),
            pltpu.VMEM((LINE, RANK, 5 * BLOCK), F32),
            pltpu.VMEM((LINE - 1, RANK, 5 * BLOCK), F32),
            pltpu.VMEM((4, RANK, 2 * BLOCK), F32),
            pltpu.VMEM((LINE - 1, RANK, 2 * BLOCK), F32),
            pltpu.VMEM((RANK, 2 * BLOCK), F32),
            pltpu.VMEM((3, RANK, 2 * BLOCK), F32),
            sems(KV_HEADS * SHARE),
            sems(4),
            sems(4),
            sems(3),
            sems(3),
            sems(LINE),
            sems(LINE),
            sems(4),
            sems(4),
            sems(3),
            sems(3),
            sems(LINE - 1),
            sems(LINE - 1),
            sems(3),
        ],
        compiler_params=pltpu.CompilerParams(
            collective_id=0, has_side_effects=True, vmem_limit_bytes=48 << 20
        ),
    )(ordering, queries[0], keys[0], values[0], grads_out[0], activations[0])
    return dq[None], dk[None], dv[None], aq, akv


def solution(mesh):
    placed = (
        P("dp", "ctx", None),
        P("dp", "ctx", None),
        P("dp", "ctx", None),
        P("dp", "ctx", None),
        P("dp", None),
        P("dp", "ctx", None),
    )
    return jax.shard_map(
        on_device,
        mesh=mesh,
        in_specs=placed,
        out_specs=(
            P("dp", "ctx", None),
            P("dp", "ctx", None),
            P("dp", "ctx", None),
            P(None, ("ctx", "dp")),
            P(None, ("ctx", "dp")),
        ),
        check_vma=False,
    )
```

time: 2290 us -> 99.6 us (0.04)
  waiting for transfers between devices: 1720 us -> 0 us
  starting transfers between devices: 188 us -> 0 us
  local copies, waits for them, and re-layouts: 177 us -> 9.26 us
  loops' own time: 98.9 us -> 0 us
  Pallas kernels: 0 us -> 89.4 us
  matrix products: 57.8 us -> 0 us
    unnamed x4 -> x0, waiting for transfers between devices: 1520 us -> none
    ppermute x60 -> x0, waiting for transfers between devices: 203 us -> none  [shifted(): lax.ppermute(value, axis, [(i, (i + by) % count) for i in range(count)])]
    ppermute x60 -> x0, starting transfers between devices: 187 us -> none  [shifted(): lax.ppermute(value, axis, [(i, (i + by) % count) for i in range(count)])]
    another operation x70 -> x0, loops' own time: 98.9 us -> none  [the longest x2 42.9 us: half_grads(): lax.scan(first_pass, start, (blocks, key_stack, value_stack))]
    pallas_call x0 -> x1, Pallas kernels: none -> 89.4 us  [on_device(): pl.pallas_call(kernel, out_shape=(jax.ShapeDtypeStruct((count, queries.sh...]
    dynamic_slice x94 -> x0, local copies, waits for them, and re-layouts: 88.5 us -> none  [the longest x64 59.5 us: half_grads(): lax.scan(first_pass, start, (blocks, key_stack, value_stack))]
    dot_general x73 -> x0, matrix products: 57.8 us -> none  [the longest x20 15.9 us: masked_scores(): jnp.einsum('thqd,lhd->hqtl', queries, keys, preferred_element_type=jnp.fl...]
    dynamic_update_slice x62 -> x0, local copies, waits for them, and re-layouts: 43.3 us -> none  [the longest x32 23.3 us: half_grads(): lax.scan(second_pass, jnp.zeros(queries.shape, jnp.float32), (blocks, key...]
  transfers between devices with their start and end apart: 62 -> 0, of which waited for: 62 -> 0; matrix products, arithmetic and copies ran while one was open for 2% -> 0% of each run, Pallas kernels for 0% -> 0%
where the time goes in v1:
time: 99.6 us; the launch traced here: 99.3 us
  Pallas kernels  89.4 us (90%)
  local copies, waits for them, and re-layouts  9.26 us (9%)
    pallas_call x1, Pallas kernels, on_device(): pl.pallas_call(kernel, out_shape=(jax.ShapeDtypeStruct((count, queries.sh...  89.4 us
    unnamed x16, local copies, waits for them, and re-layouts  9.26 us

profile of v1, /device:TPU:1, one launch (start us, length us, event | category | flops | bytes accessed | tf_op | source)
XLA Modules:
  0.0 99.3 jit_solution(12526829430127420966)
XLA Ops:
  0.6 0.8 copy.11
  1.4 0.0 copy-start.4
  1.5 0.7 copy-done.4
  2.1 0.0 copy-start
  2.1 1.2 %copy-done = bf16[1,128,4096]{2,1,0:T(8,128)(2,1)S(1)} copy-done((bf16[1,128,4096]{2,1,0:T(8,128)(2,1)S(1)}, bf16[1,128,4096]{2,1,0:T(8,128)(2,1)}, u32[]{:S(2)}) %copy-start) | copy-done | bytes 1048600
  3.3 0.0 copy-start.1
  3.3 1.2 %copy-done.1 = bf16[1,128,4096]{2,1,0:T(8,128)(2,1)S(1)} copy-done((bf16[1,128,4096]{2,1,0:T(8,128)(2,1)S(1)}, bf16[1,128,4096]{2,1,0:T(8,128)(2,1)}, u32[]{:S(2)}) %copy-start.1) | copy-done | bytes 1048600
  4.6 0.0 copy-start.2
  4.6 0.9 copy-done.2
  5.5 0.0 copy-start.3
  5.5 0.9 copy-done.3
  6.4 89.4 %shard_map.101 = (bf16[128,4096]{1,0:T(8,128)(2,1)S(1)}, bf16[128,512]{1,0:T(8,128)(2,1)S(1)}, bf16[128,512]{1,0:T(8,128)(2,1)S(1)}, f32[16,16]{1,0:T(8,128)S(1)}, f32[16,4]{1,0:T(8,128)S(1)}) custom-call(s32[1,4]{1,0:T(1,128)S(1)} %copy-done.4, bf16[128,4096]{1,0:T(8,128)(2,1)S(1)} %bitcast.9, bf16[128,512]{1,0:T(8,128)(2,1)S(1)} %bitcast.13, ...), custom_call_target="tpu_custom_call" | custom-call | tf_op jit(solution)/shard_map/pallas_call | solution.py:585
  95.8 0.7 copy.12
  96.5 1.0 copy.17
  97.4 0.7 copy.18
  98.1 0.7 copy.19
  98.7 0.6 copy.20
Async XLA Ops:
  1.4 0.7 copy-start.4
  2.1 1.2 %copy-start = (bf16[1,128,4096]{2,1,0:T(8,128)(2,1)S(1)}, bf16[1,128,4096]{2,1,0:T(8,128)(2,1)}, u32[]{:S(2)}) copy-start(bf16[1,128,4096]{2,1,0:T(8,128)(2,1)} %param.6) | copy-start | bytes 3145732
  3.3 1.2 %copy-start.1 = (bf16[1,128,4096]{2,1,0:T(8,128)(2,1)S(1)}, bf16[1,128,4096]{2,1,0:T(8,128)(2,1)}, u32[]{:S(2)}) copy-start(bf16[1,128,4096]{2,1,0:T(8,128)(2,1)} %param.9) | copy-start | bytes 3145732
  4.6 0.9 copy-start.2
  5.5 0.9 copy-start.3

commit v2 on v1

v2 whole, which is shorter than its diff:
```python
import math

import jax
import jax.numpy as jnp
from jax import lax
from jax.experimental import pallas as pl
from jax.experimental.pallas import tpu as pltpu
from jax.sharding import PartitionSpec as P

MESH = pl.DeviceIdType.MESH
F32 = jnp.float32
BF16 = jnp.bfloat16
BLOCK = 128
KV_HEADS = 4
SHARE = 8
ROWS = SHARE * BLOCK
AHEAD = 2
LINE = 8
RANK = 16
SCALE = 1.0 / math.sqrt(BLOCK)
EXP2_SCALE = SCALE / math.log(2.0)
HIDDEN = -1e30
ACT = 2 * RANK
HALF = 4 * BLOCK
EARLY = ACT + HALF
CHUNKS = ((0, ACT + 2 * BLOCK), (ACT + 2 * BLOCK, 2 * BLOCK))


def dot(a, b, a_dim, b_dim):
    return lax.dot_general(a, b, (((a_dim,), (b_dim,)), ((), ())), preferred_element_type=F32)


def kernel(
    order_ref,
    q_ref,
    k_ref,
    v_ref,
    g_ref,
    act_ref,
    dq_ref,
    dk_ref,
    dv_ref,
    aq_ref,
    akv_ref,
    own_kv,
    line_kv,
    prev_kv,
    qs,
    gs,
    acts,
    top,
    total,
    accum,
    p_low,
    s_low,
    dq_t,
    kv_terms,
    part,
    prev_part,
    next_part,
    left_out,
    left_in,
    right_out,
    right_in,
    final,
    terms,
    stage1,
    terms2,
    stage2,
    terms3,
    stage3,
    columns,
    load_sem,
    kv_sem,
    act_sem,
    g_right_e,
    g_right_l,
    g_left_e,
    g_left_l,
    g_next,
    b_prev,
    b_left_e,
    b_left_l,
    b_right_e,
    b_right_l,
    a_sem1,
    a_sem2,
    a_sem3,
):
    ctx = lax.axis_index("ctx")
    dp = lax.axis_index("dp")
    z = lax.rem(ctx, LINE)
    line = ctx // LINE
    base = line * LINE
    left = base + lax.rem(z + LINE - 1, LINE)
    right = base + lax.rem(z + 1, LINE)
    after = lax.rem(line + 1, LINE) * LINE + z
    before = lax.rem(line + LINE - 1, LINE) * LINE + z

    def copy(src, dst, sems, index, target):
        return pltpu.make_async_remote_copy(
            src_ref=src,
            dst_ref=dst,
            send_sem=sems.at[0, index],
            recv_sem=sems.at[1, index],
            device_id=target,
            device_id_type=MESH,
        )

    def slot(by):
        return lax.rem(z + by + LINE, LINE)

    def right_e(s, c, block):
        view = line_kv.at[block, pl.ds(*CHUNKS[c])]
        return copy(view, view, g_right_e, 2 * (s - 1) + c, {"ctx": right})

    def right_l(s, block):
        view = line_kv.at[block, pl.ds(EARLY, HALF)]
        return copy(view, view, g_right_l, s - 1, {"ctx": right})

    def left_e(s, c, block):
        view = line_kv.at[block, pl.ds(*CHUNKS[c])]
        return copy(view, view, g_left_e, 2 * (s - 1) + c, {"ctx": left})

    def left_l(s, block):
        view = line_kv.at[block, pl.ds(EARLY, HALF)]
        return copy(view, view, g_left_l, s - 1, {"ctx": left})

    def to_next(index, c, block):
        rows = pl.ds(*CHUNKS[c])
        return copy(
            line_kv.at[block, rows],
            prev_kv.at[block, rows],
            g_next,
            2 * index + c,
            {"ctx": after},
        )

    def to_prev(index, c):
        view = pl.ds(2 * c, 2)
        return copy(
            prev_part.at[index, view],
            next_part.at[index, view],
            b_prev,
            2 * index + c,
            {"ctx": before},
        )

    def back_left_e(s, c):
        view = pl.ds(2 * c, 2)
        return copy(
            left_out.at[s - 1, view],
            left_in.at[s - 1, view],
            b_left_e,
            2 * (s - 1) + c,
            {"ctx": left},
        )

    def back_right_e(s, c):
        view = pl.ds(2 * c, 2)
        return copy(
            right_out.at[s - 1, view],
            right_in.at[s - 1, view],
            b_right_e,
            2 * (s - 1) + c,
            {"ctx": right},
        )

    def back_left_l(s):
        return copy(
            left_out.at[s - 1, pl.ds(4, 4)],
            left_in.at[s - 1, pl.ds(4, 4)],
            b_left_l,
            s - 1,
            {"ctx": left},
        )

    def back_right_l(s):
        return copy(
            right_out.at[s - 1, pl.ds(4, 4)],
            right_in.at[s - 1, pl.ds(4, 4)],
            b_right_l,
            s - 1,
            {"ctx": right},
        )

    def load(src, dst, row, h):
        return pltpu.make_async_copy(
            src.at[:, pl.ds(h * ROWS, ROWS)], dst.at[h], load_sem.at[row, h]
        )

    def load_kv(src, which, h):
        return pltpu.make_async_copy(
            src.at[:, pl.ds(h * BLOCK, BLOCK)], own_kv.at[h, which], kv_sem.at[which, h]
        )

    barrier = pltpu.get_barrier_semaphore()
    for by in range(1, LINE):
        pl.semaphore_signal(barrier, inc=1, device_id={"ctx": base + slot(by)}, device_id_type=MESH)
        pl.semaphore_signal(
            barrier,
            inc=1,
            device_id={"ctx": lax.rem(line + by, LINE) * LINE + z},
            device_id_type=MESH,
        )
    for by in range(1, 4):
        pl.semaphore_signal(
            barrier, inc=1, device_id={"dp": lax.rem(dp + by, 4)}, device_id_type=MESH
        )

    load_act = pltpu.make_async_copy(act_ref, acts, act_sem.at[0])
    for h in range(KV_HEADS):
        load_kv(k_ref, 0, h).start()
        load_kv(v_ref, 1, h).start()
    load_act.start()

    swap = 2 * (1 - lax.rem(line, 2))
    ordering = [order_ref[0, lax.rem(j + swap, KV_HEADS)] for j in range(KV_HEADS)]
    places = []
    for h in range(KV_HEADS):
        place = jnp.int32(0)
        for j in range(1, KV_HEADS):
            place = jnp.maximum(place, jnp.where(ordering[j] == h, j, 0))
        places.append(place)

    for h in range(KV_HEADS):
        load_kv(k_ref, 0, h).wait()
        load_kv(v_ref, 1, h).wait()
    load_act.wait()
    line_kv[z, pl.ds(0, ACT), :] = acts[pl.ds(RANK, ACT), :]
    for j in range(KV_HEADS):
        first = ACT + 2 * j * BLOCK
        line_kv[z, pl.ds(first, BLOCK), :] = own_kv[ordering[j], 0]
        line_kv[z, pl.ds(first + BLOCK, BLOCK), :] = own_kv[ordering[j], 1]

    pl.semaphore_wait(barrier, 2 * (LINE - 1) + 3)
    for c in range(2):
        left_e(1, c, z).start()
        right_e(1, c, z).start()
        to_next(0, c, z).start()

    for h in range(KV_HEADS):
        load(q_ref, qs, 0, h).start()
        load(g_ref, gs, 1, h).start()

    width = 2 * BLOCK

    def name(j):
        return order_ref[0, lax.rem(j + swap, KV_HEADS)]

    def rows_of(source, j, first, count):
        heads = [source[name(j), :, pl.ds(r * BLOCK, BLOCK)] for r in range(first, first + count)]
        return jnp.concatenate(heads, axis=0)

    def scores(j, piece, keys, diagonal):
        q = rows_of(qs, j, 2 * piece, 2)
        s = dot(keys, q, 1, 1) * EXP2_SCALE
        if diagonal:
            key_at = lax.broadcasted_iota(jnp.int32, (BLOCK, width), 0)
            query_at = lax.rem(lax.broadcasted_iota(jnp.int32, (BLOCK, width), 1), BLOCK)
            own = jnp.where(key_at <= query_at, s[-BLOCK:], HIDDEN)
            s = own if s.shape[0] == BLOCK else jnp.concatenate([s[:-BLOCK], own], axis=0)
        return s

    def first_pass(j, keys, values, diagonal):
        for piece in range(ROWS // width):
            cols = pl.ds(piece * width, width)
            s = scores(j, piece, keys, diagonal)
            old = top[j, :, cols]
            new = jnp.maximum(old, jnp.max(s, axis=0, keepdims=True))
            e = jnp.exp2(s - new)
            dp_ = dot(values, rows_of(gs, j, 2 * piece, 2), 1, 1)
            factor = jnp.exp2(old - new)
            total[j, :, cols] = total[j, :, cols] * factor + jnp.sum(e, axis=0, keepdims=True)
            accum[j, :, cols] = accum[j, :, cols] * factor + jnp.sum(e * dp_, axis=0, keepdims=True)
            top[j, :, cols] = new

    def second_pass(j, keys, values, acts_k, acts_v, diagonal):
        count = keys.shape[0]
        for piece in range(ROWS // width):
            cols = pl.ds(piece * width, width)
            p = jnp.exp2(scores(j, piece, keys, diagonal) - top[j, :, cols])
            dp_ = dot(values, rows_of(gs, j, 2 * piece, 2), 1, 1)
            s_low[pl.ds(0, count), cols] = (p * (dp_ - accum[j, :, cols])).astype(BF16)
            p_low[pl.ds(0, count), cols] = p.astype(BF16)
        ds = s_low[pl.ds(0, count), :]
        dk = dot(ds, rows_of(qs, j, 0, SHARE), 1, 0)
        dv = dot(p_low[pl.ds(0, count), :], rows_of(gs, j, 0, SHARE), 1, 0)
        dq_t[j] += dot(keys, ds, 0, 0)
        kv_terms[2 * j] += dot(acts_k, dk.astype(BF16), 1, 0)
        kv_terms[2 * j + 1] += dot(acts_v, dv.astype(BF16), 1, 0)
        return dk, dv

    def keys_of(source, j, blocks):
        first = pl.multiple_of(ACT + 2 * j * BLOCK, ACT)
        keys = [source[b, pl.ds(first, BLOCK), :] for b in blocks]
        values = [source[b, pl.ds(first + BLOCK, BLOCK), :] for b in blocks]
        if len(blocks) == 1:
            return keys[0], values[0]
        return jnp.concatenate(keys, axis=0), jnp.concatenate(values, axis=0)

    def acts_of(source, blocks):
        sides = [source[b, pl.ds(0, ACT), :] for b in blocks]
        both = sides[0] if len(blocks) == 1 else jnp.concatenate(sides, axis=1)
        return both[:RANK], both[RANK:]

    def own_cases(t, run):
        far = 9 - t

        @pl.when((t == 1) & (z >= 1))
        def _():
            run((1, 0), True)

        @pl.when((t == 1) & (z == 0))
        def _():
            run((0,), True)

        @pl.when((t > 1) & (z >= far))
        def _():
            run((t, far), False)

        @pl.when((t > 1) & (z >= t) & (z < far))
        def _():
            run((t,), False)

    def prev_pair(t):
        second = jnp.where(t == 1, 0, 2 * t - 2)
        return (2 * t - 1, second), (slot(-t), lax.rem(z + t - 1, LINE))

    def own_first(t, first):
        def run(distances, diagonal):
            blocks = [slot(-d) for d in distances]

            def head(j, c):
                keys, values = keys_of(line_kv, j, blocks)
                first_pass(j, keys, values, diagonal)
                return c

            lax.fori_loop(first, first + 2, head, 0)

        own_cases(t, run)

    def prev_first(t):
        indices, blocks = prev_pair(t)
        for index, b in zip(indices, blocks):
            for c in range(2):
                to_next(index, c, b).wait_recv()

        def head(j, c):
            keys, values = keys_of(prev_kv, j, blocks)
            first_pass(j + 2, keys, values, False)
            return c

        lax.fori_loop(0, 2, head, 0)

    def early_step(t):
        block = slot(-t)
        other = slot(t)
        for c in range(2):
            left_e(t, c, other).wait_recv()

            @pl.when(t < 4)
            def _():
                left_e(t + 1, c, other).start()

            to_next(jnp.minimum(2 * t, LINE - 1), c, other).start()

            @pl.when(t < 4)
            def _():
                right_e(t, c, block).wait_recv()

                @pl.when(t < 3)
                def _():
                    right_e(t + 1, c, block).start()

                to_next(2 * t - 1, c, block).start()

    def late_step(t):
        @pl.when(z >= t)
        def _():
            @pl.when(t > 0)
            def _():
                right_l(t, slot(-t)).wait_recv()

            @pl.when((t < 4) & (z < LINE - 1))
            def _():
                right_l(t + 1, slot(-t)).start()

        @pl.when((t < 4) & (slot(t) <= 2))
        def _():
            @pl.when(t > 0)
            def _():
                left_l(t, slot(t)).wait_recv()

            @pl.when(t < 3)
            def _():
                left_l(t + 1, slot(t)).start()

    def begin():
        top[...] = jnp.full(top.shape, HIDDEN, F32)
        total[...] = jnp.zeros(total.shape, F32)
        accum[...] = jnp.zeros(accum.shape, F32)
        dq_t[...] = jnp.zeros(dq_t.shape, F32)
        kv_terms[...] = jnp.zeros(kv_terms.shape, F32)
        for d in range(LINE):
            part[d] = jnp.zeros(part.shape[1:], F32)
        for h in range(KV_HEADS):
            load(q_ref, qs, 0, h).wait()
            load(g_ref, gs, 1, h).wait()

    def gather_step(t, carry):
        early_step(t)

        @pl.when(t == 1)
        def _():
            begin()

        def halves(u, c):
            @pl.when(u == 1)
            def _():
                late_step(t)

            own_first(t, 2 * u)
            return c

        lax.fori_loop(0, 2, halves, 0)

        @pl.when(t > 1)
        def _():
            prev_first(t - 1)

        return carry

    late_step(0)
    lax.fori_loop(1, 5, gather_step, 0)

    def close_rows(first):
        heads = pl.ds(first, 2)
        top[heads] = top[heads] + jnp.log2(total[heads])
        accum[heads] = accum[heads] / total[heads]

    def own_second(t, first):
        def run(distances, diagonal):
            blocks = [slot(-d) for d in distances]
            acts_k, acts_v = acts_of(line_kv, blocks)

            def head(j, c):
                keys, values = keys_of(line_kv, j, blocks)
                dk, dv = second_pass(j, keys, values, acts_k, acts_v, diagonal)
                for i, d in enumerate(distances):
                    rows = slice(i * BLOCK, (i + 1) * BLOCK)
                    part[d, 2 * j] = dk[rows]
                    part[d, 2 * j + 1] = dv[rows]
                return c

            lax.fori_loop(first, first + 2, head, 0)

        own_cases(t, run)

    def prev_second(t):
        indices, blocks = prev_pair(t)
        acts_k, acts_v = acts_of(prev_kv, blocks)

        def head(j, c):
            keys, values = keys_of(prev_kv, j, blocks)
            dk, dv = second_pass(j + 2, keys, values, acts_k, acts_v, False)
            for i, index in enumerate(indices):
                rows = slice(i * BLOCK, (i + 1) * BLOCK)
                prev_part[index, 2 * j] = dk[rows].astype(BF16)
                prev_part[index, 2 * j + 1] = dv[rows].astype(BF16)
            return c

        lax.fori_loop(0, 2, head, 0)
        for index in indices:
            for c in range(2):
                to_prev(index, c).start()

    late = pl.ds(4, 4)

    def flush(t):
        ahead = LINE - t

        @pl.when(z >= t)
        def _():
            @pl.when((t < 4) & (z < LINE - 1))
            def _():
                back_left_l(t + 1).wait_recv()
                part[t, late] += left_in[t, late].astype(F32)

            left_out[t - 1, late] = part[t, late].astype(BF16)
            back_left_l(t).start()

        @pl.when((t < 4) & (slot(t) <= 2))
        def _():
            @pl.when(t < 3)
            def _():
                back_right_l(t + 1).wait_recv()
                part[ahead, late] += right_in[t, late].astype(F32)

            right_out[t - 1, late] = part[ahead, late].astype(BF16)
            back_right_l(t).start()

        for c in range(2):
            head = pl.ds(2 * c, 2)

            @pl.when(t < 4)
            def _():
                back_right_e(t + 1, c).wait_recv()
                part[ahead, head] += right_in[t, head].astype(F32)

            index = jnp.minimum(2 * t, LINE - 1)
            to_prev(index, c).wait_recv()
            right_out[t - 1, head] = (
                part[ahead, head] + next_part[index, head].astype(F32)
            ).astype(BF16)
            back_right_e(t, c).start()

            @pl.when(t < 4)
            def _():
                @pl.when(t < 3)
                def _():
                    back_left_e(t + 1, c).wait_recv()
                    part[t, head] += left_in[t, head].astype(F32)

                to_prev(2 * t - 1, c).wait_recv()
                left_out[t - 1, head] = (
                    part[t, head] + next_part[2 * t - 1, head].astype(F32)
                ).astype(BF16)
                back_left_e(t, c).start()

    close_rows(0)

    def early_second(i, carry):
        own_second(4 - i, 0)
        return carry

    lax.fori_loop(0, AHEAD, early_second, 0)
    prev_first(4)
    close_rows(2)

    def back_step(i, carry):
        t = 5 - i

        @pl.when(t > 1)
        def _():
            prev_second(t - 1)

        def halves(u, c):
            @pl.when((i > 0) & ((u == 1) | (i > AHEAD)))
            def _():
                own_second(t, 2 * u)

            return c

        lax.fori_loop(0, 2, halves, 0)

        @pl.when((i > 0) & (t > 1))
        def _():
            flush(t)

        return carry

    lax.fori_loop(0, 5, back_step, 0)

    for h in range(KV_HEADS):
        for r in range(SHARE):
            block = dq_t[places[h], :, pl.ds(r * BLOCK, BLOCK)] * SCALE
            dq_ref[:, pl.ds((h * SHARE + r) * BLOCK, BLOCK)] = block.astype(BF16).T
    for c in range(LINE):
        terms[c, :, pl.ds(0, 512)] = dot(
            acts[pl.ds(0, RANK), :], dq_ref[:, pl.ds(c * 512, 512)], 1, 0
        ).astype(BF16)
    for h in range(KV_HEADS):
        terms[h, :, pl.ds(512, BLOCK)] = (kv_terms[2 * places[h]] * SCALE).astype(BF16)
        terms[KV_HEADS + h, :, pl.ds(512, BLOCK)] = kv_terms[2 * places[h] + 1].astype(BF16)

    def stage1_copy(by):
        other = lax.rem(line + by, LINE)
        return copy(
            terms.at[other], stage1.at[by - 1], a_sem1, by - 1, {"ctx": other * LINE + z}
        )

    def stage2_copy(by):
        other = slot(by)
        return copy(
            terms2.at[other // 2], stage2.at[by - 1], a_sem2, by - 1, {"ctx": base + other}
        )

    def stage3_copy(by):
        return copy(terms3, stage3.at[by - 1], a_sem3, by - 1, {"dp": lax.rem(dp + by, 4)})

    for by in range(1, LINE):
        stage1_copy(by).start()
    value = terms[line].astype(F32)
    for by in range(1, LINE):
        stage1_copy(by).wait_recv()
        value = value + stage1[by - 1].astype(F32)
    for c in range(4):
        terms2[c, :, pl.ds(0, BLOCK)] = value[:, c * BLOCK : (c + 1) * BLOCK]
        terms2[c, :, pl.ds(BLOCK, BLOCK)] = value[:, 4 * BLOCK :]
    for by in range(1, LINE):
        stage2_copy(by).start()
    flush(1)
    value = terms2[z // 2]
    for by in range(1, LINE):
        stage2_copy(by).wait_recv()
        value = value + stage2[by - 1]
    terms3[...] = value
    for by in range(1, 4):
        stage3_copy(by).start()

    for c in range(2):
        head = pl.ds(2 * c, 2)
        to_prev(0, c).wait_recv()
        back_left_e(1, c).wait_recv()
        back_right_e(1, c).wait_recv()
        final[head] = (
            part[0, head]
            + next_part[0, head].astype(F32)
            + left_in[0, head].astype(F32)
            + right_in[0, head].astype(F32)
        )
    final[late] = part[0, late]

    @pl.when(z < LINE - 1)
    def _():
        back_left_l(1).wait_recv()
        final[late] += left_in[0, late].astype(F32)

    @pl.when(z <= 2)
    def _():
        back_right_l(1).wait_recv()
        final[late] += right_in[0, late].astype(F32)

    for h in range(KV_HEADS):
        span = pl.ds(h * BLOCK, BLOCK)
        dk_ref[:, span] = (final[2 * places[h]] * SCALE).astype(BF16)
        dv_ref[:, span] = final[2 * places[h] + 1].astype(BF16)

    for by in range(1, 4):
        stage3_copy(by).wait_recv()
        value = value + stage3[by - 1]
    q_first = lax.rem(z, 2) * 64 + dp * 16
    kv_first = z * 16 + dp * 4
    aq_ref[...] = pltpu.roll(value[:, :BLOCK], lax.rem(BLOCK - q_first, BLOCK), 1)[:, :RANK]
    columns[...] = value[:, BLOCK:].T
    akv_ref[...] = columns[pl.ds(kv_first, 4), :]

    for s in range(1, 5):
        for c in range(2):
            left_e(s, c, z).wait_send()
            back_right_e(s, c).wait_send()

        @pl.when((z >= s - 1) & (z < LINE - 1))
        def _():
            right_l(s, z).wait_send()

        @pl.when(z >= s)
        def _():
            back_left_l(s).wait_send()

    for s in range(1, 4):
        for c in range(2):
            right_e(s, c, z).wait_send()
            back_left_e(s, c).wait_send()

        @pl.when(slot(s - 1) <= 2)
        def _():
            left_l(s, z).wait_send()

        @pl.when(slot(s) <= 2)
        def _():
            back_right_l(s).wait_send()

    for index in range(LINE):
        for c in range(2):
            to_next(index, c, z).wait_send()
            to_prev(index, c).wait_send()
    for by in range(1, LINE):
        stage1_copy(by).wait_send()
        stage2_copy(by).wait_send()
    for by in range(1, 4):
        stage3_copy(by).wait_send()


def write_out(*refs):
    count = len(refs) // 2
    for i in range(count):
        refs[count + i][...] = refs[i][...]


def on_device(queries, keys, values, grads_out, ordering, activations):
    count = queries.shape[1]
    vmem = pl.BlockSpec(memory_space=pltpu.VMEM)
    hbm = pl.BlockSpec(memory_space=pltpu.HBM)
    pair = (2 * KV_HEADS, BLOCK, BLOCK)
    half = (KV_HEADS, BLOCK, BLOCK)

    def sems(n):
        return pltpu.SemaphoreType.DMA((2, n))

    shapes = (
        jax.ShapeDtypeStruct((count, queries.shape[2]), BF16),
        jax.ShapeDtypeStruct((count, keys.shape[2]), BF16),
        jax.ShapeDtypeStruct((count, values.shape[2]), BF16),
        jax.ShapeDtypeStruct((RANK, 16), F32),
        jax.ShapeDtypeStruct((4, RANK), F32),
    )
    results = pl.pallas_call(
        kernel,
        out_shape=shapes,
        in_specs=[pl.BlockSpec(memory_space=pltpu.SMEM)] + [hbm] * 5,
        out_specs=(vmem,) * 5,
        scratch_shapes=[
            pltpu.VMEM((KV_HEADS, 2, BLOCK, BLOCK), BF16),
            pltpu.VMEM((LINE, EARLY + HALF, BLOCK), BF16),
            pltpu.VMEM((LINE, EARLY, BLOCK), BF16),
            pltpu.VMEM((KV_HEADS, BLOCK, ROWS), BF16),
            pltpu.VMEM((KV_HEADS, BLOCK, ROWS), BF16),
            pltpu.VMEM((3 * RANK, BLOCK), BF16),
            pltpu.VMEM((KV_HEADS, 1, ROWS), F32),
            pltpu.VMEM((KV_HEADS, 1, ROWS), F32),
            pltpu.VMEM((KV_HEADS, 1, ROWS), F32),
            pltpu.VMEM((2 * BLOCK, ROWS), BF16),
            pltpu.VMEM((2 * BLOCK, ROWS), BF16),
            pltpu.VMEM((KV_HEADS, BLOCK, ROWS), F32),
            pltpu.VMEM((2 * KV_HEADS, RANK, BLOCK), F32),
            pltpu.VMEM((LINE,) + pair, F32),
            pltpu.VMEM((LINE,) + half, BF16),
            pltpu.VMEM((LINE,) + half, BF16),
            pltpu.VMEM((4,) + pair, BF16),
            pltpu.VMEM((4,) + pair, BF16),
            pltpu.VMEM((4,) + pair, BF16),
            pltpu.VMEM((4,) + pair, BF16),
            pltpu.VMEM(pair, F32),
            pltpu.VMEM((LINE, RANK, 5 * BLOCK), BF16),
            pltpu.VMEM((LINE - 1, RANK, 5 * BLOCK), BF16),
            pltpu.VMEM((4, RANK, 2 * BLOCK), F32),
            pltpu.VMEM((LINE - 1, RANK, 2 * BLOCK), F32),
            pltpu.VMEM((RANK, 2 * BLOCK), F32),
            pltpu.VMEM((3, RANK, 2 * BLOCK), F32),
            pltpu.VMEM((BLOCK, RANK), F32),
            sems(KV_HEADS),
            sems(KV_HEADS),
            pltpu.SemaphoreType.DMA((1,)),
            sems(6),
            sems(4),
            sems(8),
            sems(3),
            sems(2 * LINE),
            sems(2 * LINE),
            sems(6),
            sems(4),
            sems(8),
            sems(3),
            sems(LINE - 1),
            sems(LINE - 1),
            sems(3),
        ],
        compiler_params=pltpu.CompilerParams(
            collective_id=0, has_side_effects=True, vmem_limit_bytes=62 << 20
        ),
    )(ordering, queries[0], keys[0], values[0], grads_out[0], activations[0].T)
    dq, dk, dv, aq, akv = pl.pallas_call(
        write_out,
        out_shape=shapes,
        in_specs=[vmem] * 5,
        out_specs=(vmem,) * 5,
        compiler_params=pltpu.CompilerParams(vmem_limit_bytes=62 << 20),
    )(*results)
    return dq[None], dk[None], dv[None], aq, akv.T


def solution(mesh):
    placed = (
        P("dp", "ctx", None),
        P("dp", "ctx", None),
        P("dp", "ctx", None),
        P("dp", "ctx", None),
        P("dp", None),
        P("dp", "ctx", None),
    )
    return jax.shard_map(
        on_device,
        mesh=mesh,
        in_specs=placed,
        out_specs=(
            P("dp", "ctx", None),
            P("dp", "ctx", None),
            P("dp", "ctx", None),
            P(None, ("ctx", "dp")),
            P(None, ("ctx", "dp")),
        ),
        check_vma=False,
    )
```

time: 99.6 us -> 84.3 us (0.85)
  local copies, waits for them, and re-layouts: 9.26 us -> 0 us
  Pallas kernels: 89.4 us -> 83.4 us
    unnamed x16 -> x0, local copies, waits for them, and re-layouts: 9.26 us -> none
    pallas_call x1 -> x2, Pallas kernels: 89.4 us -> 83.4 us  [the longest x1 81 us: on_device(): pl.pallas_call(kernel, out_shape=shapes, in_specs=[pl.BlockSpec(memory_sp...]
where the time goes in v2:
time: 84.3 us; the launch traced here: 84.1 us
  Pallas kernels  83.4 us (99%)
    pallas_call x1, Pallas kernels, on_device(): pl.pallas_call(kernel, out_shape=shapes, in_specs=[pl.BlockSpec(memory_sp...  81 us
    pallas_call x1, Pallas kernels, on_device(): pl.pallas_call(write_out, out_shape=shapes, in_specs=[vmem] * 5, out_spec...  2.41 us

profile of v2, /device:TPU:1, one launch (start us, length us, event | category | flops | bytes accessed | tf_op | source)
XLA Modules:
  0.0 84.1 jit_solution(8636558236988829935)
XLA Ops:
  0.6 81.0 %shard_map.101 = (bf16[128,4096]{1,0:T(8,128)(2,1)}, bf16[128,512]{1,0:T(8,128)(2,1)}, bf16[128,512]{1,0:T(8,128)(2,1)}, f32[16,16]{1,0:T(8,128)}, f32[4,16]{1,0:T(4,128)}) custom-call(s32[1,4]{1,0:T(1,128)} %order_ref.1, bf16[128,4096]{1,0:T(8,128)(2,1)} %bitcast.11, bf16[128,512]{1,0:T(8,128)(2,1)} %bitcast.13, bf16[128,512]{1,0:T(8,128)(2,1)} %bitcast.14, ...), custom_call_target="tpu_custom_call" | custom-call | tf_op jit(solution)/shard_map/pallas_call | solution.py:709
  81.7 2.4 %shard_map.102 = (bf16[128,4096]{1,0:T(8,128)(2,1)}, bf16[128,512]{1,0:T(8,128)(2,1)}, bf16[128,512]{1,0:T(8,128)(2,1)}, f32[16,16]{1,0:T(8,128)}, f32[4,16]{1,0:T(4,128)}) custom-call(bf16[128,4096]{1,0:T(8,128)(2,1)} %get-tuple-element.15.refs_0_, bf16[128,512]{1,0:T(8,128)(2,1)} %get-tuple-element.16.refs_1_, bf16[128,512]{1,0:T(8,128)(2,1)} %get-tuple-element.17.refs_2_, ...), custom_call_target="tpu_custom_call" | custom-call | tf_op jit(solution)/shard_map/pallas_call | solution.py:764

commit v3 on v2

--- a/solution.py
+++ b/solution.py
@@ -14,7 +14,7 @@
 KV_HEADS = 4
 SHARE = 8
 ROWS = SHARE * BLOCK
-AHEAD = 2
+AHEAD = 1
 LINE = 8
 RANK = 16
 SCALE = 1.0 / math.sqrt(BLOCK)
@@ -545,6 +545,10 @@
         def _():
             prev_second(t - 1)
 
+        @pl.when((i > 1) & (t > 1))
+        def _():
+            flush(t + 1)
+
         def halves(u, c):
             @pl.when((i > 0) & ((u == 1) | (i > AHEAD)))
             def _():
@@ -554,22 +558,18 @@
 
         lax.fori_loop(0, 2, halves, 0)
 
-        @pl.when((i > 0) & (t > 1))
-        def _():
-            flush(t)
-
         return carry
 
     lax.fori_loop(0, 5, back_step, 0)
+
+    def low_block(h, r):
+        return (dq_t[places[h], :, pl.ds(r * BLOCK, BLOCK)] * SCALE).astype(BF16)
 
     for h in range(KV_HEADS):
         for r in range(SHARE):
-            block = dq_t[places[h], :, pl.ds(r * BLOCK, BLOCK)] * SCALE
-            dq_ref[:, pl.ds((h * SHARE + r) * BLOCK, BLOCK)] = block.astype(BF16).T
-    for c in range(LINE):
-        terms[c, :, pl.ds(0, 512)] = dot(
-            acts[pl.ds(0, RANK), :], dq_ref[:, pl.ds(c * 512, 512)], 1, 0
-        ).astype(BF16)
+            term = dot(acts[pl.ds(0, RANK), :], low_block(h, r), 1, 1).astype(BF16)
+            c, column = divmod(h * SHARE + r, 4)
+            terms[c, :, pl.ds(column * BLOCK, BLOCK)] = term
     for h in range(KV_HEADS):
         terms[h, :, pl.ds(512, BLOCK)] = (kv_terms[2 * places[h]] * SCALE).astype(BF16)
         terms[KV_HEADS + h, :, pl.ds(512, BLOCK)] = kv_terms[2 * places[h] + 1].astype(BF16)
@@ -591,6 +591,10 @@
 
     for by in range(1, LINE):
         stage1_copy(by).start()
+    for h in range(KV_HEADS):
+        for r in range(SHARE):
+            dq_ref[:, pl.ds((h * SHARE + r) * BLOCK, BLOCK)] = low_block(h, r).T
+    flush(2)
     value = terms[line].astype(F32)
     for by in range(1, LINE):
         stage1_copy(by).wait_recv()

time: 84.3 us -> 82.6 us (0.980)
  Pallas kernels: 83.4 us -> 81.8 us
    pallas_call x1, Pallas kernels: 81 us -> 79.4 us  [on_device(): pl.pallas_call(kernel, out_shape=shapes, in_specs=[pl.BlockSpec(memory_sp...]
where the time goes in v3:
time: 82.6 us; the launch traced here: 82.4 us
  Pallas kernels  81.8 us (99%)
    pallas_call x1, Pallas kernels, on_device(): pl.pallas_call(kernel, out_shape=shapes, in_specs=[pl.BlockSpec(memory_sp...  79.4 us
    pallas_call x1, Pallas kernels, on_device(): pl.pallas_call(write_out, out_shape=shapes, in_specs=[vmem] * 5, out_spec...  2.41 us

profile of v3, /device:TPU:1, one launch (start us, length us, event | category | flops | bytes accessed | tf_op | source)
XLA Modules:
  0.0 82.4 jit_solution(2053126166352789506)
XLA Ops:
  0.6 79.4 %shard_map.101 = (bf16[128,4096]{1,0:T(8,128)(2,1)}, bf16[128,512]{1,0:T(8,128)(2,1)}, bf16[128,512]{1,0:T(8,128)(2,1)}, f32[16,16]{1,0:T(8,128)}, f32[4,16]{1,0:T(4,128)}) custom-call(s32[1,4]{1,0:T(1,128)} %order_ref.1, bf16[128,4096]{1,0:T(8,128)(2,1)} %bitcast.11, bf16[128,512]{1,0:T(8,128)(2,1)} %bitcast.13, bf16[128,512]{1,0:T(8,128)(2,1)} %bitcast.14, ...), custom_call_target="tpu_custom_call" | custom-call | tf_op jit(solution)/shard_map/pallas_call | solution.py:713
  80.0 2.4 %shard_map.102 = (bf16[128,4096]{1,0:T(8,128)(2,1)}, bf16[128,512]{1,0:T(8,128)(2,1)}, bf16[128,512]{1,0:T(8,128)(2,1)}, f32[16,16]{1,0:T(8,128)}, f32[4,16]{1,0:T(4,128)}) custom-call(bf16[128,4096]{1,0:T(8,128)(2,1)} %get-tuple-element.15.refs_0_, bf16[128,512]{1,0:T(8,128)(2,1)} %get-tuple-element.16.refs_1_, bf16[128,512]{1,0:T(8,128)(2,1)} %get-tuple-element.17.refs_2_, ...), custom_call_target="tpu_custom_call" | custom-call | tf_op jit(solution)/shard_map/pallas_call | solution.py:768

commit v4 on v3

--- a/solution.py
+++ b/solution.py
@@ -57,6 +57,7 @@
     kv_terms,
     part,
     prev_part,
+    side_in,
     next_part,
     left_out,
     left_in,
@@ -78,6 +79,8 @@
     g_left_e,
     g_left_l,
     g_next,
+    g_side,
+    b_side,
     b_prev,
     b_left_e,
     b_left_l,
@@ -136,6 +139,20 @@
             {"ctx": after},
         )
 
+    def side_right(block):
+        view = prev_kv.at[block, pl.ds(*CHUNKS[0])]
+        return copy(view, view, g_side, 0, {"ctx": right})
+
+    def side_left(block):
+        view = prev_kv.at[block, pl.ds(*CHUNKS[1])]
+        return copy(view, view, g_side, 1, {"ctx": left})
+
+    def side_back(c):
+        index, target = ((3, left), (4, right))[c]
+        return copy(
+            prev_part.at[index, pl.ds(2 * c, 2)], side_in.at[c], b_side, c, {"ctx": target}
+        )
+
     def to_prev(index, c):
         view = pl.ds(2 * c, 2)
         return copy(
@@ -343,8 +360,24 @@
     def prev_first(t):
         indices, blocks = prev_pair(t)
         for index, b in zip(indices, blocks):
-            for c in range(2):
-                to_next(index, c, b).wait_recv()
+            for c, other in ((0, 3), (1, 4)):
+
+                @pl.when(index != other)
+                def _():
+                    to_next(index, c, b).wait_recv()
+
+        @pl.when(t == 1)
+        def _():
+            side_right(slot(-1)).start()
+
+        @pl.when(t == 2)
+        def _():
+            side_left(slot(1)).start()
+            side_right(slot(-2)).wait_recv()
+
+        @pl.when(t == 3)
+        def _():
+            side_left(slot(2)).wait_recv()
 
         def head(j, c):
             keys, values = keys_of(prev_kv, j, blocks)
@@ -363,7 +396,9 @@
             def _():
                 left_e(t + 1, c, other).start()
 
-            to_next(jnp.minimum(2 * t, LINE - 1), c, other).start()
+            @pl.when((t != 2) | (c == 0))
+            def _():
+                to_next(jnp.minimum(2 * t, LINE - 1), c, other).start()
 
             @pl.when(t < 4)
             def _():
@@ -373,7 +408,9 @@
                 def _():
                     right_e(t + 1, c, block).start()
 
-                to_next(2 * t - 1, c, block).start()
+                @pl.when((t != 2) | (c == 1))
+                def _():
+                    to_next(2 * t - 1, c, block).start()
 
     def late_step(t):
         @pl.when(z >= t)
@@ -471,9 +508,33 @@
             return c
 
         lax.fori_loop(0, 2, head, 0)
+        @pl.when(t == 3)
+        def _():
+            side_back(1).start()
+
+        @pl.when(t == 2)
+        def _():
+            side_back(0).start()
+
+        @pl.when(t == 1)
+        def _():
+            for c, index in ((1, 2), (0, 1)):
+                head_rows = pl.ds(2 * c, 2)
+                side_back(c).wait_recv()
+                prev_part[index, head_rows] = (
+                    prev_part[index, head_rows].astype(F32) + side_in[c].astype(F32)
+                ).astype(BF16)
+            to_prev(2, 1).start()
+
         for index in indices:
-            for c in range(2):
-                to_prev(index, c).start()
+            for c, skipped in ((0, (3,)), (1, (2, 4))):
+                sent = index != skipped[0]
+                for other in skipped[1:]:
+                    sent = sent & (index != other)
+
+                @pl.when(sent)
+                def _():
+                    to_prev(index, c).start()
 
     late = pl.ds(4, 4)
 
@@ -509,10 +570,13 @@
                 part[ahead, head] += right_in[t, head].astype(F32)
 
             index = jnp.minimum(2 * t, LINE - 1)
-            to_prev(index, c).wait_recv()
-            right_out[t - 1, head] = (
-                part[ahead, head] + next_part[index, head].astype(F32)
-            ).astype(BF16)
+
+            @pl.when((t != 2) | (c == 0))
+            def _():
+                to_prev(index, c).wait_recv()
+                part[ahead, head] += next_part[index, head].astype(F32)
+
+            right_out[t - 1, head] = part[ahead, head].astype(BF16)
             back_right_e(t, c).start()
 
             @pl.when(t < 4)
@@ -522,10 +586,12 @@
                     back_left_e(t + 1, c).wait_recv()
                     part[t, head] += left_in[t, head].astype(F32)
 
-                to_prev(2 * t - 1, c).wait_recv()
-                left_out[t - 1, head] = (
-                    part[t, head] + next_part[2 * t - 1, head].astype(F32)
-                ).astype(BF16)
+                @pl.when((t != 2) | (c == 1))
+                def _():
+                    to_prev(2 * t - 1, c).wait_recv()
+                    part[t, head] += next_part[2 * t - 1, head].astype(F32)
+
+                left_out[t - 1, head] = part[t, head].astype(BF16)
                 back_left_e(t, c).start()
 
     close_rows(0)
@@ -678,8 +744,13 @@
 
     for index in range(LINE):
         for c in range(2):
-            to_next(index, c, z).wait_send()
-            to_prev(index, c).wait_send()
+            if (index, c) not in ((3, 0), (4, 1)):
+                to_next(index, c, z).wait_send()
+                to_prev(index, c).wait_send()
+    side_right(z).wait_send()
+    side_left(z).wait_send()
+    side_back(0).wait_send()
+    side_back(1).wait_send()
     for by in range(1, LINE):
         stage1_copy(by).wait_send()
         stage2_copy(by).wait_send()
@@ -731,6 +802,7 @@
             pltpu.VMEM((2 * KV_HEADS, RANK, BLOCK), F32),
             pltpu.VMEM((LINE,) + pair, F32),
             pltpu.VMEM((LINE,) + half, BF16),
+            pltpu.VMEM((2, 2, BLOCK, BLOCK), BF16),
             pltpu.VMEM((LINE,) + half, BF16),
             pltpu.VMEM((4,) + pair, BF16),
             pltpu.VMEM((4,) + pair, BF16),
@@ -752,6 +824,8 @@
             sems(8),
             sems(3),
             sems(2 * LINE),
+            sems(2),
+            sems(2),
             sems(2 * LINE),
             sems(6),
             sems(4),

time: 82.6 us -> 81.4 us (0.985)
  Pallas kernels: 81.8 us -> 80.6 us
    pallas_call x1, Pallas kernels: 79.4 us -> 78.2 us  [on_device(): pl.pallas_call(kernel, out_shape=shapes, in_specs=[pl.BlockSpec(memory_sp...]
where the time goes in v4:
time: 81.4 us; the launch traced here: 81.2 us
  Pallas kernels  80.6 us (99%)
    pallas_call x1, Pallas kernels, on_device(): pl.pallas_call(kernel, out_shape=shapes, in_specs=[pl.BlockSpec(memory_sp...  78.2 us
    pallas_call x1, Pallas kernels, on_device(): pl.pallas_call(write_out, out_shape=shapes, in_specs=[vmem] * 5, out_spec...  2.41 us

profile of v4, /device:TPU:1, one launch (start us, length us, event | category | flops | bytes accessed | tf_op | source)
XLA Modules:
  0.0 81.2 jit_solution(16395839291822469992)
XLA Ops:
  0.6 78.2 %shard_map.101 = (bf16[128,4096]{1,0:T(8,128)(2,1)}, bf16[128,512]{1,0:T(8,128)(2,1)}, bf16[128,512]{1,0:T(8,128)(2,1)}, f32[16,16]{1,0:T(8,128)}, f32[4,16]{1,0:T(4,128)}) custom-call(s32[1,4]{1,0:T(1,128)} %order_ref.1, bf16[128,4096]{1,0:T(8,128)(2,1)} %bitcast.11, bf16[128,512]{1,0:T(8,128)(2,1)} %bitcast.13, bf16[128,512]{1,0:T(8,128)(2,1)} %bitcast.14, ...), custom_call_target="tpu_custom_call" | custom-call | tf_op jit(solution)/shard_map/pallas_call | solution.py:784
  78.8 2.4 %shard_map.102 = (bf16[128,4096]{1,0:T(8,128)(2,1)}, bf16[128,512]{1,0:T(8,128)(2,1)}, bf16[128,512]{1,0:T(8,128)(2,1)}, f32[16,16]{1,0:T(8,128)}, f32[4,16]{1,0:T(4,128)}) custom-call(bf16[128,4096]{1,0:T(8,128)(2,1)} %get-tuple-element.15.refs_0_, bf16[128,512]{1,0:T(8,128)(2,1)} %get-tuple-element.16.refs_1_, bf16[128,512]{1,0:T(8,128)(2,1)} %get-tuple-element.17.refs_2_, ...), custom_call_target="tpu_custom_call" | custom-call | tf_op jit(solution)/shard_map/pallas_call | solution.py:842

commit v5 on v4

--- a/solution.py
+++ b/solution.py
@@ -11,6 +11,7 @@
 F32 = jnp.float32
 BF16 = jnp.bfloat16
 BLOCK = 128
+FAR_FIRST = (4, 3, 5, 2, 6, 1, 7)
 KV_HEADS = 4
 SHARE = 8
 ROWS = SHARE * BLOCK
@@ -655,7 +656,7 @@
     def stage3_copy(by):
         return copy(terms3, stage3.at[by - 1], a_sem3, by - 1, {"dp": lax.rem(dp + by, 4)})
 
-    for by in range(1, LINE):
+    for by in FAR_FIRST:
         stage1_copy(by).start()
     for h in range(KV_HEADS):
         for r in range(SHARE):
@@ -668,7 +669,7 @@
     for c in range(4):
         terms2[c, :, pl.ds(0, BLOCK)] = value[:, c * BLOCK : (c + 1) * BLOCK]
         terms2[c, :, pl.ds(BLOCK, BLOCK)] = value[:, 4 * BLOCK :]
-    for by in range(1, LINE):
+    for by in FAR_FIRST:
         stage2_copy(by).start()
     flush(1)
     value = terms2[z // 2]

time: 81.4 us -> 81.9 us (level)
  no operation moved by 1% of the time
where the time goes in v5:
time: 81.9 us; the launch traced here: 81.7 us
  Pallas kernels  81 us (99%)
    pallas_call x1, Pallas kernels, on_device(): pl.pallas_call(kernel, out_shape=shapes, in_specs=[pl.BlockSpec(memory_sp...  78.6 us
    pallas_call x1, Pallas kernels, on_device(): pl.pallas_call(write_out, out_shape=shapes, in_specs=[vmem] * 5, out_spec...  2.41 us

profile of v5, /device:TPU:1, one launch (start us, length us, event | category | flops | bytes accessed | tf_op | source)
XLA Modules:
  0.0 81.7 jit_solution(4405948688476386336)
XLA Ops:
  0.6 78.6 %shard_map.101 = (bf16[128,4096]{1,0:T(8,128)(2,1)}, bf16[128,512]{1,0:T(8,128)(2,1)}, bf16[128,512]{1,0:T(8,128)(2,1)}, f32[16,16]{1,0:T(8,128)}, f32[4,16]{1,0:T(4,128)}) custom-call(s32[1,4]{1,0:T(1,128)} %order_ref.1, bf16[128,4096]{1,0:T(8,128)(2,1)} %bitcast.11, bf16[128,512]{1,0:T(8,128)(2,1)} %bitcast.13, bf16[128,512]{1,0:T(8,128)(2,1)} %bitcast.14, ...), custom_call_target="tpu_custom_call" | custom-call | tf_op jit(solution)/shard_map/pallas_call | solution.py:785
  79.3 2.4 %shard_map.102 = (bf16[128,4096]{1,0:T(8,128)(2,1)}, bf16[128,512]{1,0:T(8,128)(2,1)}, bf16[128,512]{1,0:T(8,128)(2,1)}, f32[16,16]{1,0:T(8,128)}, f32[4,16]{1,0:T(4,128)}) custom-call(bf16[128,4096]{1,0:T(8,128)(2,1)} %get-tuple-element.15.refs_0_, bf16[128,512]{1,0:T(8,128)(2,1)} %get-tuple-element.16.refs_1_, bf16[128,512]{1,0:T(8,128)(2,1)} %get-tuple-element.17.refs_2_, ...), custom_call_target="tpu_custom_call" | custom-call | tf_op jit(solution)/shard_map/pallas_call | solution.py:843
